TPU v7x, 32 devices: a whole 2x2x4 slice. The times are simulated.
32 devices in a mesh: outer: 4 (over y, x), inner: 8 (over z, core).
Axes of the slice: x: 2, y: 2, z: 4, core: 2. Of those that a mesh axis runs over, the one named last changes fastest.
Arguments:
- jacobians: float32 [32, 256, 256], P(('outer', 'inner')), may hold values from -1 to 1, as said below
- weights: float32 [32, 256, 256], P(('outer', 'inner')), may hold values from -3 to 3, as said below
Outputs:
- transitions: float32 [32, 256, 256], P(('outer', 'inner'))
- gramians: float32 [4, 256, 256], P('outer', 'inner')
Inputs may be any that keep to these rules, and one draw needn't show every extreme that they name: `jacobians`: each Jacobian's singular values lie within one percent of 1. `weights`: each weight matrix is symmetric.
All inputs are finite; a program needn't handle non-finite values.
Results may differ from a plain program's by a relative error of at most 0.0003.
Values sent between devices are 32-bit elements; how exact they have to be, the bound alone decides.
A program may use at most 64 MiB of HBM per device.

v0:
```python
import jax
import jax.numpy as jnp
from jax import lax
from jax.sharding import PartitionSpec as P


def carried_in(x, axis, combine, identity):
    count, position = (lax.axis_size(axis), lax.axis_index(axis))
    everything = lax.all_gather(x, axis)
    start = jnp.broadcast_to(jnp.asarray(identity, x.dtype), x.shape)

    def turn(k, before):
        reached = k < position
        new = combine(before, everything[k])
        return jnp.where(reached, new, before)

    return lax.fori_loop(0, count, turn, start)


def spread(block, axis, holder):
    block = jnp.where(lax.axis_index(axis) == holder, block, jnp.zeros_like(block))
    return lax.psum(block, axis)


def matmul(left, right):
    return jnp.dot(left, right, precision=lax.Precision.HIGHEST, preferred_element_type=jnp.float32)


def combine(earlier, later):
    return matmul(later, earlier)


def shards(jacobians, weights):
    order = jacobians.shape[1]
    identity = jnp.eye(order, dtype=jnp.float32)
    running = identity
    step = 0
    running = matmul(jacobians[step], running)
    local_chain = [running]
    inside = carried_in(running, "inner", combine, identity)
    closing = matmul(running, inside)
    whole = spread(closing, "inner", lax.axis_size("inner") - 1)
    segment_start = carried_in(whole, "outer", combine, identity)
    step = 0
    relative = matmul(local_chain[step], inside)
    inner_total = matmul(matmul(relative.T, weights[step]), relative)
    total = matmul(matmul(segment_start.T, inner_total), segment_start)
    before = matmul(inside, segment_start)
    outputs = [matmul(local_chain[0], before)]
    transitions = jnp.stack(outputs, axis=0)
    share = lax.psum_scatter(total, "inner", scatter_dimension=0, tiled=True)
    return (transitions, share[None])


def solution(mesh):
    return jax.shard_map(
        shards,
        mesh=mesh,
        in_specs=(P(("outer", "inner"), None, None), P(("outer", "inner"), None, None)),
        out_specs=(P(("outer", "inner"), None, None), P("outer", "inner", None)),
        check_vma=False,
    )
```

profile of v0, /device:TPU:0, one launch (start us, length us, event | category | flops | bytes accessed | tf_op | source)
XLA Modules:
  0.0 175.4 jit_solution(15853961294155427568)
XLA Ops:
  7.2 0.0 copy-start
  7.2 0.0 all-gather.6.cloned.1.call-start
  7.2 0.9 copy-done
  8.1 1.0 fusion.8
  9.2 0.0 all-gather.6.cloned.1.call-update
  9.2 0.0 all-reduce.2.cloned.1.call-start
  9.3 32.7 %all-gather.6.cloned.1.call-done = f32[2048,256]{0,1:T(8,128)} async-done(((f32[256,256]{0,1:T(8,128)}), f32[2048,256]{0,1:T(8,128)}) %all-gather.6.cloned.1.call-update) | async-done | bytes 2097168 | tf_op jit(solution)/shard_map/all_gather | solution.py:9
  42.0 1.9 %copy.6 = f32[2048,256]{1,0:T(8,128)S(1)} copy(f32[2048,256]{0,1:T(8,128)} %all-gather.6.cloned.1.call-done) | data formatting | bytes 4194304 | tf_op jit(solution)/shard_map/while | solution.py:17
  44.0 0.0 copy-start.1
  44.0 0.0 copy-start.2
  44.0 3.5 %while.26 = (s32[]{:T(128)}, f32[256,256]{1,0:T(8,128)S(1)}, s32[]{:T(128)}, f32[8,256,256]{2,1,0:T(8,128)S(1)}, s32[]{:T(128)}) while((s32[]{:T(128)}, f32[256,256]{1,0:T(8,128)S(1)}, s32[]{:T(128)}, f32[8,256,256]{2,1,0:T(8,128)S(1)}, s32[]{:T(128)}) %tuple.71), condition=%wide.region_1.2_spmd, body=%wide.region_0.1_spmd.sunk | while | flops 201392128 | bytes 1572939 | solution.py:17
  44.0 0.4 convolution_select_fusion.4
  44.5 0.4 convolution_select_fusion.4
  44.9 0.4 convolution_select_fusion.4
  45.3 0.4 convolution_select_fusion.4
  45.8 0.4 convolution_select_fusion.4
  46.2 0.4 convolution_select_fusion.4
  46.7 0.4 convolution_select_fusion.4
  47.1 0.4 convolution_select_fusion.4
  47.5 0.0 copy-done.1
  47.5 0.6 fusion.13
  48.1 0.7 select_bitcast_fusion
  48.8 0.0 all-reduce.2.cloned.1.call-update
  48.9 0.0 all-gather.4.cloned.1.call-start
  48.9 54.5 %all-reduce.2.cloned.1.call-done = f32[1,256,256]{2,1,0:T(8,128)} async-done(((f32[1,256,256]{2,1,0:T(8,128)}), f32[1,256,256]{2,1,0:T(8,128)}) %all-reduce.2.cloned.1.call-update) | async-done | bytes 262160 | tf_op jit(solution)/shard_map/psum | solution.py:22
  103.4 0.0 all-gather.4.cloned.1.call-update
  103.4 0.0 reduce-scatter.2.cloned.1.call-start
  103.5 0.0 copy-done.2
  103.5 0.6 fusion.6
  104.1 0.4 fusion.15
  104.5 26.6 %all-gather.4.cloned.1.call-done = f32[4,256,256]{2,1,0:T(8,128)} async-done(((f32[1,256,256]{2,1,0:T(8,128)}), f32[4,256,256]{2,1,0:T(8,128)}) %all-gather.4.cloned.1.call-update) | async-done | bytes 1048592 | tf_op jit(solution)/shard_map/all_gather | solution.py:9
  131.1 5.5 %while.27 = (s32[]{:T(128)}, f32[256,256]{1,0:T(8,128)S(1)}, s32[]{:T(128)}, f32[4,256,256]{2,1,0:T(8,128)}, s32[]{:T(128)}) while((s32[]{:T(128)}, f32[256,256]{1,0:T(8,128)S(1)}, s32[]{:T(128)}, f32[4,256,256]{2,1,0:T(8,128)}, s32[]{:T(128)}) %tuple.60), condition=%wide.region_4.5_spmd, body=%wide.region_3.4_spmd.sunk | while | flops 201392128 | bytes 1573447 | solution.py:17
  131.1 1.3 convolution_select_fusion.5
  132.5 1.3 convolution_select_fusion.5
  133.9 1.3 convolution_select_fusion.5
  135.3 1.3 convolution_select_fusion.5
  136.6 0.6 fusion.16
  137.2 1.1 fusion.17
  138.3 0.0 reduce-scatter.2.cloned.1.call-update
  138.3 0.4 fusion.14
  138.7 1.3 convolution_bitcast_fusion
  140.0 28.9 %reduce-scatter.2.cloned.1.call-done = f32[32,256]{1,0:T(8,128)} async-done(((f32[256,256]{1,0:T(8,128)}), f32[32,256]{1,0:T(8,128)}) %reduce-scatter.2.cloned.1.call-update) | async-done | bytes 32784 | tf_op jit(solution)/shard_map/reduce_scatter | solution.py:51
  (14 shorter events, 0.3 us)
Async XLA Ops:
  7.2 1.0 copy-start
  7.2 34.8 %all-gather.6.cloned.1.call-start = ((), (), s32[]{:S(2)}) async-start(), calls=%async_computation.4 | async-start | bytes 2359296 | tf_op jit(solution)/shard_map/all_gather | solution.py:9
  9.2 94.2 %all-reduce.2.cloned.1.call-start = ((), (), s32[]{:S(2)}) async-start(), calls=%async_computation.1 | async-start | bytes 524288 | tf_op jit(solution)/shard_map/psum | solution.py:22
  44.0 3.6 %copy-start.1 = (f32[256,256]{1,0:T(8,128)S(1)}, f32[256,256]{1,0:T(8,128)}, u32[]{:S(2)}) copy-start(f32[256,256]{1,0:T(8,128)} %fusion.8) | copy-start | bytes 786436
  44.0 59.5 %copy-start.2 = (f32[1,256,256]{2,1,0:T(8,128)S(1)}, f32[1,256,256]{2,1,0:T(8,128)}, u32[]{:S(2)}) copy-start(f32[1,256,256]{2,1,0:T(8,128)} %param.7) | copy-start | bytes 786436
  48.9 82.2 %all-gather.4.cloned.1.call-start = ((), (), s32[]{:S(2)}) async-start(), calls=%async_computation.2 | async-start | bytes 1310720 | tf_op jit(solution)/shard_map/all_gather | solution.py:9
  103.4 65.4 %reduce-scatter.2.cloned.1.call-start = ((), (), s32[]{:S(2)}) async-start(), calls=%async_computation.3 | async-start | bytes 294912 | tf_op jit(solution)/shard_map/reduce_scatter | solution.py:51
Sparse Core Ops, SparseCore 0:
  10.2 31.7 all-gather.5
  49.0 54.3 all-reduce.1
  105.4 25.5 all-gather.3
  138.4 30.4 reduce-scatter.1
where the time goes:
time: 176 us; the launch traced here: 175 us
  waiting for transfers between devices  143 us (81%)
  matrix products  14.4 us (8%)
  between operations  13.9 us (8%)
  local copies, waits for them, and re-layouts  3.08 us (2%)
    all_gather x2, waiting for transfers between devices, carried_in(): everything = lax.all_gather(x, axis)  59.3 us
    psum x1, waiting for transfers between devices, spread(): return lax.psum(block, axis)  54.5 us
    reduce_scatter x1, waiting for transfers between devices, shards(): share = lax.psum_scatter(total, 'inner', scatter_dimension=0, tiled=True)  28.9 us
    dot_general x20, matrix products, matmul(): jnp.dot(left, right, precision=lax.Precision.HIGHEST, preferred_element_t...  14.4 us
  transfers between devices with their start and end apart: 4, of which 4 were waited for; matrix products, arithmetic and copies ran while one was open for 2% of the time, Pallas kernels for 0%

commit v1 on v0

v1 whole, which is shorter than its diff:
```python
import functools

import jax
import jax.numpy as jnp
from jax import lax
from jax.experimental import pallas as pl
from jax.experimental.pallas import tpu as pltpu
from jax.sharding import PartitionSpec as P

MESH = pl.DeviceIdType.MESH
CHUNKS = 2


def split(x):
    high = x.astype(jnp.bfloat16)
    return high, (x - high.astype(jnp.float32)).astype(jnp.bfloat16)


def product(left, right, dims=((1,), (0,))):
    dot = functools.partial(
        lax.dot_general, dimension_numbers=(dims, ((), ())), preferred_element_type=jnp.float32
    )
    return dot(left[0], right[0]) + (dot(left[0], right[1]) + dot(left[1], right[0]))


def log2(n):
    return n.bit_length() - 1


def kernel(n_outer, n_inner, jac_hbm, weight_hbm, trans_ref, gram_ref,
           total, other, prefix, weight, term, terms,
           load_sem, send_sem, recv_sem, pass_send, pass_recv, term_send, term_recv):
    outer, inner = lax.axis_index("outer"), lax.axis_index("inner")
    order = prefix.shape[0]
    half = order // 2
    piece = half // CHUNKS
    core = lax.rem(inner, 2)
    sibling = inner + 1 - 2 * core
    load_jac = pltpu.make_async_copy(jac_hbm.at[0], total.at[0], load_sem.at[0])
    load_weight = pltpu.make_async_copy(weight_hbm.at[0], weight, load_sem.at[1])
    load_jac.start()
    load_weight.start()

    def partner(index, bit):
        side = lax.rem(index // (1 << bit), 2)
        return side, index + (1 - 2 * side) * (1 << bit)

    steps = [("inner", b) for b in range(1, log2(n_inner))] + [("outer", b) for b in range(log2(n_outer))]
    barrier = pltpu.get_barrier_semaphore()
    for d in range(1, n_inner):
        pl.semaphore_signal(barrier, inc=1, device_id={"inner": lax.rem(inner + d, n_inner)}, device_id_type=MESH)
    for b in range(log2(n_outer)):
        pl.semaphore_signal(barrier, inc=1, device_id={"outer": partner(outer, b)[1]}, device_id_type=MESH)
    pl.semaphore_wait(barrier, n_inner - 1 + log2(n_outer))

    load_jac.wait()
    swap = pltpu.make_async_remote_copy(
        total.at[0], other.at[0], pass_send.at[0, 0], pass_recv.at[0, 0], {"inner": sibling}, MESH)
    swap.start()
    prefix[...] = total[0]
    swap.wait()
    pending = []

    def exchange(s, side, target, last):
        mine = pl.ds(pl.multiple_of(core * half, half), half)
        theirs = pl.ds(pl.multiple_of((1 - core) * half, half), half)

        @pl.when(side == 1)
        def _():
            right = split(other[s])
            if not last:
                total[s + 1, mine] = product(split(total[s, mine]), right)

        @pl.when(side == 0)
        def _():
            if not last:
                total[s + 1, mine] = product(split(other[s, mine]), split(total[s]))

        copies = []
        if not last:
            for c in range(CHUNKS):
                rows = pl.ds(pl.multiple_of(core * half + c * piece, piece), piece)
                copy = pltpu.make_async_remote_copy(
                    total.at[s + 1, rows], other.at[s + 1, rows],
                    send_sem.at[s + 1, c], recv_sem.at[s + 1, c], target, MESH)
                copy.start()
                copies.append((copy, rows))

        @pl.when(side == 1)
        def _():
            right = split(other[s])
            if not last:
                total[s + 1, theirs] = product(split(total[s, theirs]), right)
            prefix[...] = product(split(prefix[...]), right)

        @pl.when(side == 0)
        def _():
            if not last:
                total[s + 1, theirs] = product(split(other[s, theirs]), split(total[s]))

        passes = []
        for c, (copy, rows) in enumerate(copies):
            copy.wait_recv()
            onward = pltpu.make_async_remote_copy(
                other.at[s + 1, rows], other.at[s + 1, rows],
                pass_send.at[s + 1, c], pass_recv.at[s + 1, c], {"inner": sibling}, MESH)
            onward.start()
            passes.append(onward)
        for onward in passes:
            onward.wait_recv()
        pending.extend(copy for copy, _ in copies)
        pending.extend(passes)

    sides = [core]
    targets = []
    for axis, b in steps:
        side, index = partner(inner if axis == "inner" else outer, b)
        sides.append(side)
        targets.append({axis: index})
    for s in range(len(steps) + 1):
        last = s == len(steps)
        exchange(s, sides[s], None if last else targets[s], last)

    trans_ref[0] = prefix[...]
    current = split(prefix[...])
    load_weight.wait()
    term[...] = product(current, split(product(split(weight[...]), current)), ((0,), (0,)))
    share = order // n_inner
    copies = []
    for d in range(1, n_inner):
        owner = lax.rem(inner + d, n_inner)
        copy = pltpu.make_async_remote_copy(
            term.at[pl.ds(pl.multiple_of(owner * share, share), share)], terms.at[d],
            term_send.at[d], term_recv.at[d], {"inner": owner}, MESH)
        copy.start()
        copies.append(copy)
    result = term[pl.ds(pl.multiple_of(inner * share, share), share)]
    for d in range(1, n_inner):
        copies[d - 1].wait_recv()
        result = result + terms[d]
    gram_ref[0] = result
    for copy in copies + pending:
        copy.wait_send()


def shards(n_outer, n_inner, jacobians, weights):
    order = jacobians.shape[1]
    share = order // n_inner
    levels = log2(n_inner) + log2(n_outer)
    square = (order, order)
    f32 = jnp.float32
    dma = pltpu.SemaphoreType.DMA
    return pl.pallas_call(
        functools.partial(kernel, n_outer, n_inner),
        out_shape=(jax.ShapeDtypeStruct((1,) + square, f32), jax.ShapeDtypeStruct((1, share, order), f32)),
        in_specs=[pl.BlockSpec(memory_space=pl.ANY)] * 2,
        out_specs=[pl.BlockSpec(memory_space=pltpu.VMEM)] * 2,
        scratch_shapes=[
            pltpu.VMEM((levels,) + square, f32),
            pltpu.VMEM((levels,) + square, f32),
            pltpu.VMEM(square, f32),
            pltpu.VMEM(square, f32),
            pltpu.VMEM(square, f32),
            pltpu.VMEM((n_inner, share, order), f32),
            dma((2,)),
            dma((levels, CHUNKS)),
            dma((levels, CHUNKS)),
            dma((levels, CHUNKS)),
            dma((levels, CHUNKS)),
            dma((n_inner,)),
            dma((n_inner,)),
        ],
        compiler_params=pltpu.CompilerParams(
            collective_id=0, has_side_effects=True, vmem_limit_bytes=32 * 1024 * 1024),
    )(jacobians, weights)


def solution(mesh):
    return jax.shard_map(
        functools.partial(shards, mesh.shape["outer"], mesh.shape["inner"]),
        mesh=mesh,
        in_specs=(P(("outer", "inner"), None, None), P(("outer", "inner"), None, None)),
        out_specs=(P(("outer", "inner"), None, None), P("outer", "inner", None)),
        check_vma=False,
    )
```

time: 176 us -> 44.6 us (0.25)
  waiting for transfers between devices: 143 us -> 0 us
  Pallas kernels: 0 us -> 40.5 us
  matrix products: 14.4 us -> 0 us
  between operations: 13.9 us -> 0.65 us
    all_gather x2 -> x0, waiting for transfers between devices: 59.3 us -> none  [carried_in(): everything = lax.all_gather(x, axis)]
    psum x1 -> x0, waiting for transfers between devices: 54.5 us -> none  [spread(): return lax.psum(block, axis)]
    pallas_call x0 -> x1, Pallas kernels: none -> 40.5 us  [shards(): pl.pallas_call(functools.partial(kernel, n_outer, n_inner), out_shape=(ja...]
    reduce_scatter x1 -> x0, waiting for transfers between devices: 28.9 us -> none  [shards(): share = lax.psum_scatter(total, 'inner', scatter_dimension=0, tiled=True)]
    dot_general x20 -> x0, matrix products: 14.4 us -> none  [matmul(): jnp.dot(left, right, precision=lax.Precision.HIGHEST, preferred_element_t...]
    unnamed x7 -> x6, local copies, waits for them, and re-layouts: 0.93 us -> 3.21 us
    while x13 -> x0, local copies, waits for them, and re-layouts: 2.15 us -> none  [the longest x1 1.92 us: carried_in(): return lax.fori_loop(0, count, turn, start)]
  transfers between devices with their start and end apart: 4 -> 0, of which waited for: 4 -> 0; matrix products, arithmetic and copies ran while one was open for 2% -> 0% of each run, Pallas kernels for 0% -> 0%
where the time goes in v1:
time: 44.6 us; the launch traced here: 44.3 us
  Pallas kernels  40.5 us (91%)
  local copies, waits for them, and re-layouts  3.21 us (7%)
  between operations  0.65 us (1%)
    pallas_call x1, Pallas kernels, shards(): pl.pallas_call(functools.partial(kernel, n_outer, n_inner), out_shape=(ja...  40.5 us
    unnamed x6, local copies, waits for them, and re-layouts  3.21 us

profile of v1, /device:TPU:0, one launch (start us, length us, event | category | flops | bytes accessed | tf_op | source)
XLA Modules:
  0.0 44.3 jit_solution(15278219158948945810)
XLA Ops:
  0.6 0.0 copy-start
  0.6 0.9 %copy-done = f32[1,256,256]{2,1,0:T(8,128)S(1)} copy-done((f32[1,256,256]{2,1,0:T(8,128)S(1)}, f32[1,256,256]{2,1,0:T(8,128)}, u32[]{:S(2)}) %copy-start) | copy-done | bytes 262168
  1.6 0.0 copy-start.1
  1.6 0.9 %copy-done.1 = f32[1,256,256]{2,1,0:T(8,128)S(1)} copy-done((f32[1,256,256]{2,1,0:T(8,128)S(1)}, f32[1,256,256]{2,1,0:T(8,128)}, u32[]{:S(2)}) %copy-start.1) | copy-done | bytes 262168
  2.5 40.5 %shard_map.41 = (f32[1,256,256]{2,1,0:T(8,128)S(1)}, f32[1,32,256]{2,1,0:T(8,128)S(1)}) custom-call(f32[1,256,256]{2,1,0:T(8,128)S(1)} %copy-done, f32[1,256,256]{2,1,0:T(8,128)S(1)} %copy-done.1), custom_call_target="tpu_custom_call" | custom-call | tf_op jit(solution)/shard_map/pallas_call | solution.py:153
  43.0 0.7 %copy.6 = f32[1,256,256]{2,1,0:T(8,128)} copy(f32[1,256,256]{2,1,0:T(8,128)S(1)} %get-tuple-element.4) | data formatting | bytes 524288
  43.7 0.6 %copy.7 = f32[1,32,256]{2,1,0:T(8,128)} copy(f32[1,32,256]{2,1,0:T(8,128)S(1)} %get-tuple-element.5) | data formatting | bytes 65536
Async XLA Ops:
  0.6 1.0 %copy-start = (f32[1,256,256]{2,1,0:T(8,128)S(1)}, f32[1,256,256]{2,1,0:T(8,128)}, u32[]{:S(2)}) copy-start(f32[1,256,256]{2,1,0:T(8,128)} %jac_hbm.1) | copy-start | bytes 786436
  1.6 0.9 %copy-start.1 = (f32[1,256,256]{2,1,0:T(8,128)S(1)}, f32[1,256,256]{2,1,0:T(8,128)}, u32[]{:S(2)}) copy-start(f32[1,256,256]{2,1,0:T(8,128)} %weight_hbm.1) | copy-start | bytes 786436

commit v2 on v1

v2 whole, which is shorter than its diff:
```python
import functools

import jax
import jax.numpy as jnp
from jax import lax
from jax.experimental import pallas as pl
from jax.experimental.pallas import tpu as pltpu
from jax.sharding import PartitionSpec as P

MESH = pl.DeviceIdType.MESH


def split(x):
    high = x.astype(jnp.bfloat16)
    return high, (x - high.astype(jnp.float32)).astype(jnp.bfloat16)


def product(left, right, dims=((1,), (0,))):
    dot = functools.partial(
        lax.dot_general, dimension_numbers=(dims, ((), ())), preferred_element_type=jnp.float32
    )
    return dot(left[0], right[0]) + (dot(left[0], right[1]) + dot(left[1], right[0]))


def log2(n):
    return n.bit_length() - 1


def kernel(n_outer, n_inner, jac_hbm, weight_hbm, trans_ref, gram_ref,
           total, other, prefix, weight, term, terms, summed, starts, start,
           load_sem, send_sem, recv_sem, pass_send, pass_recv, term_send, term_recv, sum_send, sum_recv,
           start_send, start_recv, start_pass_send, start_pass_recv):
    outer, inner = lax.axis_index("outer"), lax.axis_index("inner")
    order = prefix.shape[0]
    half = order // 2
    core = lax.rem(inner, 2)
    sibling = inner + 1 - 2 * core
    load_jac = pltpu.make_async_copy(jac_hbm.at[0], total.at[0], load_sem.at[0])
    load_weight = pltpu.make_async_copy(weight_hbm.at[0], weight, load_sem.at[1])
    load_jac.start()
    load_weight.start()

    def partner(index, bit):
        side = lax.rem(index // (1 << bit), 2)
        return side, index + (1 - 2 * side) * (1 << bit)

    steps = [("inner", b) for b in range(1, log2(n_inner))]
    barrier = pltpu.get_barrier_semaphore()
    for d in range(1, n_inner):
        pl.semaphore_signal(barrier, inc=1, device_id={"inner": lax.rem(inner + d, n_inner)}, device_id_type=MESH)
    for d in range(1, n_outer):
        pl.semaphore_signal(barrier, inc=1, device_id={"outer": lax.rem(outer + d, n_outer)}, device_id_type=MESH)
    pl.semaphore_wait(barrier, n_inner + n_outer - 2)

    load_jac.wait()
    swap = pltpu.make_async_remote_copy(
        total.at[0], other.at[0], pass_send.at[0], pass_recv.at[0], {"inner": sibling}, MESH)
    swap.start()
    prefix[...] = total[0]
    swap.wait()
    pending = []

    mine = pl.ds(pl.multiple_of(core * half, half), half)
    theirs = pl.ds(pl.multiple_of((1 - core) * half, half), half)
    share = order // n_inner

    def to_segment(d):
        return pltpu.make_async_remote_copy(
            total.at[len(steps) + 1, mine], starts.at[d, mine], start_send.at[d], start_recv.at[d],
            {"outer": lax.rem(outer + d, n_outer)}, MESH)

    def to_sibling(d):
        return pltpu.make_async_remote_copy(
            starts.at[d, mine], starts.at[d, mine], start_pass_send.at[d], start_pass_recv.at[d],
            {"inner": sibling}, MESH)

    def to_owner(d):
        owner = lax.rem(inner + d, n_inner)
        return pltpu.make_async_remote_copy(
            term.at[pl.ds(pl.multiple_of(owner * share, share), share)], terms.at[d],
            term_send.at[d], term_recv.at[d], {"inner": owner}, MESH)

    own = pl.ds(pl.multiple_of(inner * share, share), share)

    def to_all(d):
        return pltpu.make_async_remote_copy(
            summed.at[own], summed.at[own], sum_send.at[d], sum_recv.at[d],
            {"inner": lax.rem(inner + d, n_inner)}, MESH)

    sides = [core] + [partner(inner, b)[0] for _, b in steps]
    targets = [{axis: partner(inner, b)[1]} for axis, b in steps]
    for s in range(len(steps) + 1):
        side, last = sides[s], s == len(steps)

        @pl.when(side == 1)
        def _():
            total[s + 1, mine] = product(split(total[s, mine]), split(other[s]))

        @pl.when(side == 0)
        def _():
            total[s + 1, mine] = product(split(other[s, mine]), split(total[s]))

        if last:
            for d in range(1, n_outer):
                @pl.when(outer + d < n_outer)
                def _(d=d):
                    to_segment(d).start()
        else:
            copy = pltpu.make_async_remote_copy(
                total.at[s + 1, mine], other.at[s + 1, mine], send_sem.at[s + 1], recv_sem.at[s + 1],
                targets[s], MESH)
            copy.start()

        @pl.when(side == 1)
        def _():
            right = split(other[s])
            if not last:
                total[s + 1, theirs] = product(split(total[s, theirs]), right)
            prefix[...] = product(split(prefix[...]), right)

        if not last:
            @pl.when(side == 0)
            def _():
                total[s + 1, theirs] = product(split(other[s, theirs]), split(total[s]))

            copy.wait_recv()
            onward = pltpu.make_async_remote_copy(
                other.at[s + 1, mine], other.at[s + 1, mine], pass_send.at[s + 1], pass_recv.at[s + 1],
                {"inner": sibling}, MESH)
            onward.start()
            onward.wait_recv()
            pending.extend((copy, onward))

    current = split(prefix[...])
    load_weight.wait()
    term[...] = product(current, split(product(split(weight[...]), current)), ((0,), (0,)))
    owners = [to_owner(d) for d in range(1, n_inner)]
    for copy in owners:
        copy.start()
    for d in range(1, n_outer):
        @pl.when(outer >= d)
        def _(d=d):
            to_segment(d).wait_recv()
            to_sibling(d).start()
    result = term[own]
    for d in range(1, n_inner):
        owners[d - 1].wait_recv()
        result = result + terms[d]
    summed[own] = result
    everyone = [to_all(d) for d in range(1, n_inner)]
    for copy in everyone:
        copy.start()

    for d in range(1, n_outer):
        @pl.when(outer >= d)
        def _(d=d):
            to_sibling(d).wait_recv()
            if d == 1:
                start[...] = starts[d]
            else:
                start[...] = product(split(start[...]), split(starts[d]))

    @pl.when(outer == 0)
    def _():
        trans_ref[0] = prefix[...]

    @pl.when(outer > 0)
    def _():
        trans_ref[0] = product(split(prefix[...]), split(start[...]))

    for copy in everyone:
        copy.wait_recv()
    for copy in owners:
        copy.wait_send()

    @pl.when(outer == 0)
    def _():
        gram_ref[0] = summed[own]

    @pl.when(outer > 0)
    def _():
        first = split(start[...])
        term[...] = product(first, split(product(split(summed[...]), first)), ((0,), (0,)))
        gram_ref[0] = term[own]

    for copy in pending + everyone:
        copy.wait_send()
    for d in range(1, n_outer):
        @pl.when(outer + d < n_outer)
        def _(d=d):
            to_segment(d).wait_send()

        @pl.when(outer >= d)
        def _(d=d):
            to_sibling(d).wait_send()


def shards(n_outer, n_inner, jacobians, weights):
    order = jacobians.shape[1]
    share = order // n_inner
    levels = log2(n_inner)
    square = (order, order)
    f32 = jnp.float32
    dma = pltpu.SemaphoreType.DMA
    return pl.pallas_call(
        functools.partial(kernel, n_outer, n_inner),
        out_shape=(jax.ShapeDtypeStruct((1,) + square, f32), jax.ShapeDtypeStruct((1, share, order), f32)),
        in_specs=[pl.BlockSpec(memory_space=pl.ANY)] * 2,
        out_specs=[pl.BlockSpec(memory_space=pltpu.VMEM)] * 2,
        scratch_shapes=[
            pltpu.VMEM((levels + 1,) + square, f32),
            pltpu.VMEM((levels,) + square, f32),
            pltpu.VMEM(square, f32),
            pltpu.VMEM(square, f32),
            pltpu.VMEM(square, f32),
            pltpu.VMEM((n_inner, share, order), f32),
            pltpu.VMEM(square, f32),
            pltpu.VMEM((n_outer,) + square, f32),
            pltpu.VMEM(square, f32),
            dma((2,)),
            dma((levels,)),
            dma((levels,)),
            dma((levels,)),
            dma((levels,)),
            dma((n_inner,)),
            dma((n_inner,)),
            dma((n_inner,)),
            dma((n_inner,)),
            dma((n_outer,)),
            dma((n_outer,)),
            dma((n_outer,)),
            dma((n_outer,)),
        ],
        compiler_params=pltpu.CompilerParams(
            collective_id=0, has_side_effects=True, vmem_limit_bytes=56 * 1024 * 1024),
    )(jacobians, weights)


def solution(mesh):
    return jax.shard_map(
        functools.partial(shards, mesh.shape["outer"], mesh.shape["inner"]),
        mesh=mesh,
        in_specs=(P(("outer", "inner"), None, None), P(("outer", "inner"), None, None)),
        out_specs=(P(("outer", "inner"), None, None), P("outer", "inner", None)),
        check_vma=False,
    )
```

time: 44.6 us -> 40 us (0.90)
  the two profiles are of different devices: /device:TPU:0 before, /device:TPU:15 now
where the time goes in v2:
time: 40 us; the launch traced here: 39.9 us
  Pallas kernels  36.9 us (92%)
  local copies, waits for them, and re-layouts  2.29 us (6%)
  between operations  0.65 us (2%)
    pallas_call x1, Pallas kernels, shards(): pl.pallas_call(functools.partial(kernel, n_outer, n_inner), out_shape=(ja...  36.9 us
    unnamed x4, local copies, waits for them, and re-layouts  2.29 us

profile of v2, /device:TPU:15, one launch (start us, length us, event | category | flops | bytes accessed | tf_op | source)
XLA Modules:
  0.0 39.9 jit_solution(15875692513968518898)
XLA Ops:
  0.6 36.9 %shard_map.41 = (f32[1,256,256]{2,1,0:T(8,128)}, f32[1,32,256]{2,1,0:T(8,128)}) custom-call(f32[1,256,256]{2,1,0:T(8,128)} %jac_hbm.1, f32[1,256,256]{2,1,0:T(8,128)} %weight_hbm.1), custom_call_target="tpu_custom_call" | custom-call | tf_op jit(solution)/shard_map/pallas_call | solution.py:205
  37.5 0.0 copy-start
  37.6 1.7 %copy.6 = f32[1,256,256]{2,1,0:T(8,128)} copy(f32[1,256,256]{2,1,0:T(8,128)} %get-tuple-element.4) | data formatting | bytes 524288
  39.2 0.0 copy-done
  39.2 0.6 %copy.7 = f32[1,32,256]{2,1,0:T(8,128)} copy(f32[1,32,256]{2,1,0:T(8,128)S(1)} %copy-done) | data formatting | bytes 65536
Async XLA Ops:
  37.5 1.7 %copy-start = (f32[1,32,256]{2,1,0:T(8,128)S(1)}, f32[1,32,256]{2,1,0:T(8,128)}, u32[]{:S(2)}) copy-start(f32[1,32,256]{2,1,0:T(8,128)} %get-tuple-element.5) | copy-start | bytes 98308

commit v3 on v2

--- a/solution.py
+++ b/solution.py
@@ -27,8 +27,9 @@
 
 
 def kernel(n_outer, n_inner, jac_hbm, weight_hbm, trans_ref, gram_ref,
-           total, other, prefix, weight, term, terms, summed, starts, start,
+           total, other, prefix, weight, term, terms, joined, summed, starts, start,
            load_sem, send_sem, recv_sem, pass_send, pass_recv, term_send, term_recv, sum_send, sum_recv,
+           sum_pass_send, sum_pass_recv,
            start_send, start_recv, start_pass_send, start_pass_recv):
     outer, inner = lax.axis_index("outer"), lax.axis_index("inner")
     order = prefix.shape[0]
@@ -58,7 +59,6 @@
     swap.start()
     prefix[...] = total[0]
     swap.wait()
-    pending = []
 
     mine = pl.ds(pl.multiple_of(core * half, half), half)
     theirs = pl.ds(pl.multiple_of((1 - core) * half, half), half)
@@ -74,31 +74,100 @@
             starts.at[d, mine], starts.at[d, mine], start_pass_send.at[d], start_pass_recv.at[d],
             {"inner": sibling}, MESH)
 
+    chips = n_inner // 2
+    piece = half // chips
+    own = pl.ds(pl.multiple_of(inner * share, share), share)
+
+    def rows_of(chip):
+        return pl.ds(pl.multiple_of(core * half + chip * piece, piece), piece)
+
+    def chip_at(d):
+        return lax.rem(inner // 2 + d, chips)
+
     def to_owner(d):
-        owner = lax.rem(inner + d, n_inner)
-        return pltpu.make_async_remote_copy(
-            term.at[pl.ds(pl.multiple_of(owner * share, share), share)], terms.at[d],
-            term_send.at[d], term_recv.at[d], {"inner": owner}, MESH)
-
-    own = pl.ds(pl.multiple_of(inner * share, share), share)
+        return pltpu.make_async_remote_copy(
+            term.at[rows_of(chip_at(d))], terms.at[d], term_send.at[d], term_recv.at[d],
+            {"inner": chip_at(d) * 2 + core}, MESH)
+
+    kept = rows_of(chip_at(0))
 
     def to_all(d):
         return pltpu.make_async_remote_copy(
-            summed.at[own], summed.at[own], sum_send.at[d], sum_recv.at[d],
-            {"inner": lax.rem(inner + d, n_inner)}, MESH)
+            summed.at[kept], summed.at[kept], sum_send.at[d], sum_recv.at[d],
+            {"inner": chip_at(d) * 2 + core}, MESH)
+
+    def sum_to_sibling(d):
+        rows = rows_of(chip_at(chips - d))
+        return pltpu.make_async_remote_copy(
+            summed.at[rows], summed.at[rows], sum_pass_send.at[d], sum_pass_recv.at[d],
+            {"inner": sibling}, MESH)
 
     sides = [core] + [partner(inner, b)[0] for _, b in steps]
     targets = [{axis: partner(inner, b)[1]} for axis, b in steps]
+    left_columns = pl.ds(pl.multiple_of(core * half, half), half)
+    right_columns = pl.ds(pl.multiple_of((1 - core) * half, half), half)
+
+    def hop(source, target, s, by_row, device, send, recv):
+        part = (s, mine) if by_row else (s, slice(None), left_columns)
+        return pltpu.make_async_remote_copy(
+            source.at[part], target.at[part], send.at[s], recv.at[s], device, MESH)
+
+    def on_kind(kind, act):
+        @pl.when(kind == 0)
+        def _():
+            act(True)
+
+        @pl.when(kind == 1)
+        def _():
+            act(False)
+
+    def send_half(s, kind):
+        on_kind(kind, lambda by_row: hop(total, other, s, by_row, targets[s - 1], send_sem, recv_sem).start())
+
+    def pass_half(s, kind):
+        def act(by_row):
+            hop(total, other, s, by_row, targets[s - 1], send_sem, recv_sem).wait_recv()
+            hop(other, other, s, by_row, {"inner": sibling}, pass_send, pass_recv).start()
+        on_kind(kind, act)
+
+    def wait_pass(s, kind):
+        on_kind(kind, lambda by_row: hop(
+            other, other, s, by_row, {"inner": sibling}, pass_send, pass_recv).wait_recv())
+
+    def join_rows(s, side, rows):
+        @pl.when(side == 1)
+        def _():
+            total[s + 1, rows] = product(split(total[s, rows]), split(other[s]))
+
+        @pl.when(side == 0)
+        def _():
+            total[s + 1, rows] = product(split(other[s, rows]), split(total[s]))
+
+    def join_early(side, mine, columns):
+        @pl.when(side == 1)
+        def _():
+            total[2, :, columns] = product(split(total[1]), split(other[1, :, columns]))
+
+        @pl.when(side == 0)
+        def _():
+            total[2, mine] = product(split(other[1, mine]), split(total[1]))
+
+    kinds = [None, sides[1] if len(sides) > 1 else None]
+    for s in range(2, len(sides)):
+        kinds.append(sides[1] * 1 if s == 2 else inner * 0)
+    def sent(s):
+        return 1 - kinds[s] if s == 1 else kinds[s]
+
     for s in range(len(steps) + 1):
         side, last = sides[s], s == len(steps)
-
-        @pl.when(side == 1)
-        def _():
-            total[s + 1, mine] = product(split(total[s, mine]), split(other[s]))
-
-        @pl.when(side == 0)
-        def _():
-            total[s + 1, mine] = product(split(other[s, mine]), split(total[s]))
+        early = s == 1 and not last
+        if early:
+            join_early(side, mine, left_columns)
+        elif s == 0 and not last:
+            join_rows(s, side, mine)
+            join_rows(s, side, theirs)
+        else:
+            join_rows(s, side, mine)
 
         if last:
             for d in range(1, n_outer):
@@ -106,50 +175,52 @@
                 def _(d=d):
                     to_segment(d).start()
         else:
-            copy = pltpu.make_async_remote_copy(
-                total.at[s + 1, mine], other.at[s + 1, mine], send_sem.at[s + 1], recv_sem.at[s + 1],
-                targets[s], MESH)
-            copy.start()
+            send_half(s + 1, sent(s + 1))
+
+        if early:
+            wait_pass(s, kinds[s])
+            join_early(side, theirs, right_columns)
+        elif not last and s > 0:
+            join_rows(s, side, theirs)
 
         @pl.when(side == 1)
         def _():
-            right = split(other[s])
-            if not last:
-                total[s + 1, theirs] = product(split(total[s, theirs]), right)
-            prefix[...] = product(split(prefix[...]), right)
+            prefix[...] = product(split(prefix[...]), split(other[s]))
 
         if not last:
-            @pl.when(side == 0)
-            def _():
-                total[s + 1, theirs] = product(split(other[s, theirs]), split(total[s]))
-
-            copy.wait_recv()
-            onward = pltpu.make_async_remote_copy(
-                other.at[s + 1, mine], other.at[s + 1, mine], pass_send.at[s + 1], pass_recv.at[s + 1],
-                {"inner": sibling}, MESH)
-            onward.start()
-            onward.wait_recv()
-            pending.extend((copy, onward))
+            pass_half(s + 1, kinds[s + 1])
+            if s + 1 != 1 or s + 1 == len(steps):
+                wait_pass(s + 1, kinds[s + 1])
 
     current = split(prefix[...])
     load_weight.wait()
     term[...] = product(current, split(product(split(weight[...]), current)), ((0,), (0,)))
-    owners = [to_owner(d) for d in range(1, n_inner)]
+    join = pltpu.make_async_remote_copy(
+        term.at[theirs], joined, term_send.at[0], term_recv.at[0], {"inner": sibling}, MESH)
+    join.start()
+    join.wait_recv()
+    term[mine] = term[mine] + joined[...]
+    owners = [to_owner(d) for d in range(1, chips)]
     for copy in owners:
         copy.start()
+    result = term[kept]
+    for d in range(1, chips):
+        owners[d - 1].wait_recv()
+        result = result + terms[d]
+    summed[kept] = result
+    everyone = [to_all(d) for d in range(1, chips)]
+    for copy in everyone:
+        copy.start()
+    onward = [sum_to_sibling(d) for d in range(chips)]
+    onward[0].start()
     for d in range(1, n_outer):
         @pl.when(outer >= d)
         def _(d=d):
             to_segment(d).wait_recv()
             to_sibling(d).start()
-    result = term[own]
-    for d in range(1, n_inner):
-        owners[d - 1].wait_recv()
-        result = result + terms[d]
-    summed[own] = result
-    everyone = [to_all(d) for d in range(1, n_inner)]
-    for copy in everyone:
-        copy.start()
+    for d in range(1, chips):
+        everyone[d - 1].wait_recv()
+        onward[d].start()
 
     for d in range(1, n_outer):
         @pl.when(outer >= d)
@@ -168,9 +239,9 @@
     def _():
         trans_ref[0] = product(split(prefix[...]), split(start[...]))
 
-    for copy in everyone:
+    for copy in onward:
         copy.wait_recv()
-    for copy in owners:
+    for copy in owners + [join]:
         copy.wait_send()
 
     @pl.when(outer == 0)
@@ -183,8 +254,17 @@
         term[...] = product(first, split(product(split(summed[...]), first)), ((0,), (0,)))
         gram_ref[0] = term[own]
 
-    for copy in pending + everyone:
+    for copy in everyone + onward:
         copy.wait_send()
+
+    def finish(s):
+        on_kind(sent(s), lambda by_row: hop(
+            total, other, s, by_row, targets[s - 1], send_sem, recv_sem).wait_send())
+        on_kind(kinds[s], lambda by_row: hop(
+            other, other, s, by_row, {"inner": sibling}, pass_send, pass_recv).wait_send())
+
+    for s in range(1, len(sides)):
+        finish(s)
     for d in range(1, n_outer):
         @pl.when(outer + d < n_outer)
         def _(d=d):
@@ -213,7 +293,8 @@
             pltpu.VMEM(square, f32),
             pltpu.VMEM(square, f32),
             pltpu.VMEM(square, f32),
-            pltpu.VMEM((n_inner, share, order), f32),
+            pltpu.VMEM((n_inner // 2, order // n_inner, order), f32),
+            pltpu.VMEM((order // 2, order), f32),
             pltpu.VMEM(square, f32),
             pltpu.VMEM((n_outer,) + square, f32),
             pltpu.VMEM(square, f32),
@@ -222,10 +303,12 @@
             dma((levels,)),
             dma((levels,)),
             dma((levels,)),
-            dma((n_inner,)),
-            dma((n_inner,)),
-            dma((n_inner,)),
-            dma((n_inner,)),
+            dma((n_inner // 2,)),
+            dma((n_inner // 2,)),
+            dma((n_inner // 2,)),
+            dma((n_inner // 2,)),
+            dma((n_inner // 2,)),
+            dma((n_inner // 2,)),
             dma((n_outer,)),
             dma((n_outer,)),
             dma((n_outer,)),

time: 40 us -> 37.3 us (0.932)
  the two profiles are of different devices: /device:TPU:15 before, /device:TPU:0 now
where the time goes in v3:
time: 37.3 us; the launch traced here: 37.2 us
  Pallas kernels  34.2 us (92%)
  local copies, waits for them, and re-layouts  2.29 us (6%)
  between operations  0.65 us (2%)
    pallas_call x1, Pallas kernels, shards(): pl.pallas_call(functools.partial(kernel, n_outer, n_inner), out_shape=(ja...  34.2 us
    unnamed x4, local copies, waits for them, and re-layouts  2.29 us

profile of v3, /device:TPU:0, one launch (start us, length us, event | category | flops | bytes accessed | tf_op | source)
XLA Modules:
  0.0 37.2 jit_solution(5222093018704902948)
XLA Ops:
  0.6 34.2 %shard_map.41 = (f32[1,256,256]{2,1,0:T(8,128)}, f32[1,32,256]{2,1,0:T(8,128)}) custom-call(f32[1,256,256]{2,1,0:T(8,128)} %jac_hbm.1, f32[1,256,256]{2,1,0:T(8,128)} %weight_hbm.1), custom_call_target="tpu_custom_call" | custom-call | tf_op jit(solution)/shard_map/pallas_call | solution.py:285
  34.9 0.0 copy-start
  34.9 1.7 %copy.6 = f32[1,256,256]{2,1,0:T(8,128)} copy(f32[1,256,256]{2,1,0:T(8,128)} %get-tuple-element.4) | data formatting | bytes 524288
  36.5 0.0 copy-done
  36.5 0.6 %copy.7 = f32[1,32,256]{2,1,0:T(8,128)} copy(f32[1,32,256]{2,1,0:T(8,128)S(1)} %copy-done) | data formatting | bytes 65536
Async XLA Ops:
  34.9 1.7 %copy-start = (f32[1,32,256]{2,1,0:T(8,128)S(1)}, f32[1,32,256]{2,1,0:T(8,128)}, u32[]{:S(2)}) copy-start(f32[1,32,256]{2,1,0:T(8,128)} %get-tuple-element.5) | copy-start | bytes 98308

commit v4 on v3

--- a/solution.py
+++ b/solution.py
@@ -27,7 +27,7 @@
 
 
 def kernel(n_outer, n_inner, jac_hbm, weight_hbm, trans_ref, gram_ref,
-           total, other, prefix, weight, term, terms, joined, summed, starts, start,
+           total, other, prefix, weight, term, terms, joined, inside, reduced, summed, starts, start,
            load_sem, send_sem, recv_sem, pass_send, pass_recv, term_send, term_recv, sum_send, sum_recv,
            sum_pass_send, sum_pass_recv,
            start_send, start_recv, start_pass_send, start_pass_recv):
@@ -47,11 +47,12 @@
 
     steps = [("inner", b) for b in range(1, log2(n_inner))]
     barrier = pltpu.get_barrier_semaphore()
-    for d in range(1, n_inner):
-        pl.semaphore_signal(barrier, inc=1, device_id={"inner": lax.rem(inner + d, n_inner)}, device_id_type=MESH)
+    pl.semaphore_signal(barrier, inc=1, device_id={"inner": sibling}, device_id_type=MESH)
+    for d in range(1, n_inner // 2):
+        pl.semaphore_signal(barrier, inc=1, device_id={"inner": lax.rem(inner + 2 * d, n_inner)}, device_id_type=MESH)
     for d in range(1, n_outer):
         pl.semaphore_signal(barrier, inc=1, device_id={"outer": lax.rem(outer + d, n_outer)}, device_id_type=MESH)
-    pl.semaphore_wait(barrier, n_inner + n_outer - 2)
+    pl.semaphore_wait(barrier, n_inner // 2 + n_outer - 1)
 
     load_jac.wait()
     swap = pltpu.make_async_remote_copy(
@@ -86,7 +87,7 @@
 
     def to_owner(d):
         return pltpu.make_async_remote_copy(
-            term.at[rows_of(chip_at(d))], terms.at[d], term_send.at[d], term_recv.at[d],
+            reduced.at[rows_of(chip_at(d))], terms.at[d], term_send.at[d], term_recv.at[d],
             {"inner": chip_at(d) * 2 + core}, MESH)
 
     kept = rows_of(chip_at(0))
@@ -104,6 +105,10 @@
 
     sides = [core] + [partner(inner, b)[0] for _, b in steps]
     targets = [{axis: partner(inner, b)[1]} for axis, b in steps]
+    join = pltpu.make_async_remote_copy(
+        term, joined, term_send.at[0], term_recv.at[0], {"inner": sibling}, MESH)
+    row = lax.broadcasted_iota(jnp.int32, (order, order), 0)
+    inside[...] = (row == lax.broadcasted_iota(jnp.int32, (order, order), 1)).astype(jnp.float32)
     left_columns = pl.ds(pl.multiple_of(core * half, half), half)
     right_columns = pl.ds(pl.multiple_of((1 - core) * half, half), half)
 
@@ -183,27 +188,30 @@
         elif not last and s > 0:
             join_rows(s, side, theirs)
 
+        gathered = prefix if s == 0 else inside
+
         @pl.when(side == 1)
         def _():
-            prefix[...] = product(split(prefix[...]), split(other[s]))
+            gathered[...] = product(split(gathered[...]), split(other[s]))
+
+        if s == 0:
+            current = split(prefix[...])
+            load_weight.wait()
+            term[...] = product(current, split(product(split(weight[...]), current)), ((0,), (0,)))
+            join.start()
 
         if not last:
             pass_half(s + 1, kinds[s + 1])
             if s + 1 != 1 or s + 1 == len(steps):
                 wait_pass(s + 1, kinds[s + 1])
 
-    current = split(prefix[...])
-    load_weight.wait()
-    term[...] = product(current, split(product(split(weight[...]), current)), ((0,), (0,)))
-    join = pltpu.make_async_remote_copy(
-        term.at[theirs], joined, term_send.at[0], term_recv.at[0], {"inner": sibling}, MESH)
-    join.start()
     join.wait_recv()
-    term[mine] = term[mine] + joined[...]
+    current = split(inside[...])
+    reduced[...] = product(current, split(product(split(term[...] + joined[...]), current)), ((0,), (0,)))
     owners = [to_owner(d) for d in range(1, chips)]
     for copy in owners:
         copy.start()
-    result = term[kept]
+    result = reduced[kept]
     for d in range(1, chips):
         owners[d - 1].wait_recv()
         result = result + terms[d]
@@ -233,11 +241,12 @@
 
     @pl.when(outer == 0)
     def _():
-        trans_ref[0] = prefix[...]
+        trans_ref[0] = product(split(prefix[...]), split(inside[...]))
 
     @pl.when(outer > 0)
     def _():
-        trans_ref[0] = product(split(prefix[...]), split(start[...]))
+        before = product(split(inside[...]), split(start[...]))
+        trans_ref[0] = product(split(prefix[...]), split(before))
 
     for copy in onward:
         copy.wait_recv()
@@ -294,7 +303,9 @@
             pltpu.VMEM(square, f32),
             pltpu.VMEM(square, f32),
             pltpu.VMEM((n_inner // 2, order // n_inner, order), f32),
-            pltpu.VMEM((order // 2, order), f32),
+            pltpu.VMEM(square, f32),
+            pltpu.VMEM(square, f32),
+            pltpu.VMEM(square, f32),
             pltpu.VMEM(square, f32),
             pltpu.VMEM((n_outer,) + square, f32),
             pltpu.VMEM(square, f32),

time: 37.3 us -> 36.6 us (0.981)
  Pallas kernels: 34.2 us -> 33.6 us
    pallas_call x1, Pallas kernels: 34.2 us -> 33.6 us  [shards(): pl.pallas_call(functools.partial(kernel, n_outer, n_inner), out_shape=(ja...]
where the time goes in v4:
time: 36.6 us; the launch traced here: 36.5 us
  Pallas kernels  33.6 us (92%)
  local copies, waits for them, and re-layouts  2.29 us (6%)
  between operations  0.65 us (2%)
    pallas_call x1, Pallas kernels, shards(): pl.pallas_call(functools.partial(kernel, n_outer, n_inner), out_shape=(ja...  33.6 us
    unnamed x4, local copies, waits for them, and re-layouts  2.29 us

profile of v4, /device:TPU:0, one launch (start us, length us, event | category | flops | bytes accessed | tf_op | source)
XLA Modules:
  0.0 36.5 jit_solution(2470558504518832065)
XLA Ops:
  0.6 33.6 %shard_map.41 = (f32[1,256,256]{2,1,0:T(8,128)}, f32[1,32,256]{2,1,0:T(8,128)}) custom-call(f32[1,256,256]{2,1,0:T(8,128)} %jac_hbm.1, f32[1,256,256]{2,1,0:T(8,128)} %weight_hbm.1), custom_call_target="tpu_custom_call" | custom-call | tf_op jit(solution)/shard_map/pallas_call | solution.py:294
  34.2 0.0 copy-start
  34.2 1.7 %copy.6 = f32[1,256,256]{2,1,0:T(8,128)} copy(f32[1,256,256]{2,1,0:T(8,128)} %get-tuple-element.4) | data formatting | bytes 524288
  35.9 0.0 copy-done
  35.9 0.6 %copy.7 = f32[1,32,256]{2,1,0:T(8,128)} copy(f32[1,32,256]{2,1,0:T(8,128)S(1)} %copy-done) | data formatting | bytes 65536
Async XLA Ops:
  34.2 1.7 %copy-start = (f32[1,32,256]{2,1,0:T(8,128)S(1)}, f32[1,32,256]{2,1,0:T(8,128)}, u32[]{:S(2)}) copy-start(f32[1,32,256]{2,1,0:T(8,128)} %get-tuple-element.5) | copy-start | bytes 98308

commit v5 on v4

--- a/solution.py
+++ b/solution.py
@@ -171,15 +171,10 @@
         elif s == 0 and not last:
             join_rows(s, side, mine)
             join_rows(s, side, theirs)
-        else:
+        elif not last:
             join_rows(s, side, mine)
 
-        if last:
-            for d in range(1, n_outer):
-                @pl.when(outer + d < n_outer)
-                def _(d=d):
-                    to_segment(d).start()
-        else:
+        if not last:
             send_half(s + 1, sent(s + 1))
 
         if early:
@@ -211,6 +206,11 @@
     owners = [to_owner(d) for d in range(1, chips)]
     for copy in owners:
         copy.start()
+    join_rows(len(steps), sides[-1], mine)
+    for d in range(1, n_outer):
+        @pl.when(outer + d < n_outer)
+        def _(d=d):
+            to_segment(d).start()
     result = reduced[kept]
     for d in range(1, chips):
         owners[d - 1].wait_recv()

time: 36.6 us -> 36.4 us (level)
  no operation moved by 1% of the time
where the time goes in v5:
time: 36.4 us; the launch traced here: 36.3 us
  Pallas kernels  33.3 us (91%)
  local copies, waits for them, and re-layouts  2.29 us (6%)
  between operations  0.65 us (2%)
    pallas_call x1, Pallas kernels, shards(): pl.pallas_call(functools.partial(kernel, n_outer, n_inner), out_shape=(ja...  33.3 us
    unnamed x4, local copies, waits for them, and re-layouts  2.29 us

profile of v5, /device:TPU:0, one launch (start us, length us, event | category | flops | bytes accessed | tf_op | source)
XLA Modules:
  0.0 36.3 jit_solution(16447980964179148868)
XLA Ops:
  0.6 33.3 %shard_map.41 = (f32[1,256,256]{2,1,0:T(8,128)}, f32[1,32,256]{2,1,0:T(8,128)}) custom-call(f32[1,256,256]{2,1,0:T(8,128)} %jac_hbm.1, f32[1,256,256]{2,1,0:T(8,128)} %weight_hbm.1), custom_call_target="tpu_custom_call" | custom-call | tf_op jit(solution)/shard_map/pallas_call | solution.py:294
  34.0 0.0 copy-start
  34.0 1.7 %copy.6 = f32[1,256,256]{2,1,0:T(8,128)} copy(f32[1,256,256]{2,1,0:T(8,128)} %get-tuple-element.4) | data formatting | bytes 524288
  35.6 0.0 copy-done
  35.6 0.6 %copy.7 = f32[1,32,256]{2,1,0:T(8,128)} copy(f32[1,32,256]{2,1,0:T(8,128)S(1)} %copy-done) | data formatting | bytes 65536
Async XLA Ops:
  34.0 1.7 %copy-start = (f32[1,32,256]{2,1,0:T(8,128)S(1)}, f32[1,32,256]{2,1,0:T(8,128)}, u32[]{:S(2)}) copy-start(f32[1,32,256]{2,1,0:T(8,128)} %get-tuple-element.5) | copy-start | bytes 98308
